TPU v7x, 512 devices: a whole 4x8x8 slice. The times are simulated.
512 devices in a mesh: tm: 128 (over y, z, core), space: 4 (over x).
Axes of the slice: x: 4, y: 8, z: 8, core: 2. Of those that a mesh axis runs over, the one named last changes fastest.
Arguments:
- u_coarse_guess: float32 [1024, 32, 1024], P('tm', 'space'), may hold values from -6 to 6
- forcing: float32 [2048, 32, 1024], P('tm', 'space'), may hold values from -6 to 6
- u_init: float32 [32, 1024], P('space'), may hold values from -6 to 6
- diffuse: float32 [32, 1024], P('space'), may hold values from 0.01 to 0.03
- vel_x: float32 [32, 1024], P('space'), may hold values from -0.05 to 0.05
- vel_y: float32 [32, 1024], P('space'), may hold values from -0.05 to 0.05
- react: float32 [32, 1024], P('space'), may hold values from 0.0002 to 0.02
Outputs:
- u_next: float32 [2048, 32, 1024], P('tm', 'space')
All inputs are finite; a program needn't handle non-finite values.
Results may differ from a plain program's by a relative error of at most 0.00013.
Values sent between devices are 32-bit elements; how exact they have to be, the bound alone decides.
A program may use at most 64 MiB of HBM per device.

v0:
```python
import functools

import jax
import jax.numpy as jnp
from jax import lax
from jax.experimental import pallas as pl
from jax.experimental.pallas import tpu as pltpu
from jax.sharding import PartitionSpec as P

MESH = pl.DeviceIdType.MESH
GROUP = 16
PAD = 8
DEPTH = 6


def add_squares(x):
    zero = None
    out = []
    for m in range(len(x) + 2):
        terms = []
        if m < len(x):
            terms.append(x[m])
        if 1 <= m <= len(x):
            terms.append(2.0 * x[m - 1])
        if 2 <= m <= len(x) + 1:
            terms.append(x[m - 2])
        total = terms[0]
        for t in terms[1:]:
            total = total + t
        out.append(total)
    del zero
    return out


def kernel(
    slabs,
    strips,
    guess,
    force,
    init,
    diffuse,
    vel_x,
    vel_y,
    react,
    out,
    gx,
    fx,
    hx,
    cx,
    wx,
    decx,
    px,
    dx,
    zx,
    rx,
    tx,
    ex,
    ob,
    ini,
    g7,
    d7,
    sp,
    dp,
    r1,
    pre,
    pw,
    r2,
    wo,
    ce,
    cex,
    lsem,
    es,
    er,
    ss,
    sr,
):
    tm = lax.axis_index("tm")
    sx = lax.axis_index("space")
    y = tm // GROUP
    q = lax.rem(tm, GROUP)
    count = slabs * GROUP
    xs = (lax.rem(sx + 1, strips), lax.rem(sx + strips - 1, strips))
    nxt = lax.rem(tm + 1, count)
    prv = lax.rem(tm + count - 1, count)
    last = tm == count - 1
    cols = ob.shape[2]
    own = pl.ds(PAD, 8)

    barrier = pltpu.get_barrier_semaphore()
    peers = [(tm, s) for s in xs]
    for t in (nxt, prv):
        peers += [(t, s) for s in (sx,) + xs]
    for m in range(1, GROUP):
        t = y * GROUP + lax.rem(q + m, GROUP)
        peers += [(t, s) for s in (sx,) + xs]
    for m in range(1, slabs):
        peers.append((lax.rem(y + m, slabs) * GROUP + q, sx))
    for dev in peers:
        pl.semaphore_signal(barrier, inc=1, device_id=dev, device_id_type=MESH)

    loads = []
    for i, (src, dst) in enumerate(
        [
            (guess, gx.at[pl.ds(1, 8), own]),
            (force.at[:, 0], fx.at[:, own]),
            (force.at[:, 1], hx),
            (init, ini),
            (diffuse, cx.at[0, own]),
            (vel_x, cx.at[1, own]),
            (vel_y, cx.at[2, own]),
            (react, cx.at[3, own]),
        ]
    ):
        cp = pltpu.make_async_copy(src, dst, lsem.at[i])
        cp.start()
        loads.append(cp)
    for cp in loads:
        cp.wait()

    sent = []
    slot = [0]

    def send(src, dst, dev):
        i = slot[0]
        slot[0] += 1
        cp = pltpu.make_async_remote_copy(
            src_ref=src,
            dst_ref=dst,
            send_sem=ss.at[i],
            recv_sem=sr.at[i],
            device_id=dev,
            device_id_type=MESH,
        )
        cp.start()
        sent.append(cp)
        return cp

    def halo(ref, lead, h):
        a = send(ref.at[lead + (pl.ds(16 - h, h),)], ref.at[lead + (pl.ds(8 - h, h),)], (tm, xs[0]))
        b = send(ref.at[lead + (pl.ds(8, h),)], ref.at[lead + (pl.ds(16, h),)], (tm, xs[1]))
        return [a, b]

    def onward(src, ref, lead, h):
        return [
            send(src, ref.at[lead + (own,)], (nxt, sx)),
            send(src.at[pl.ds(8 - h, h)], ref.at[lead + (pl.ds(8 - h, h),)], (nxt, xs[0])),
            send(src.at[pl.ds(0, h)], ref.at[lead + (pl.ds(16, h),)], (nxt, xs[1])),
        ]

    def change(G, F, H, k):
        return (G[k - 1] + F[k] + H[k] - G[k], 2.0 * G[k - 1] + F[k], G[k - 1])

    def reader(ref, lane, shift, padded):
        def read(k):
            if padded:
                return ref[k + shift, own, lane]
            return ref[k + shift, :, lane]

        class Reader:
            def __getitem__(self, k):
                return read(k)

        return Reader()

    def fields(lane):
        return reader(gx, lane, 1, True), reader(fx, lane, 0, True), reader(hx, lane, 0, False)

    def first(lane):
        G, F, H = fields(lane)
        d0, d1, d2 = [jnp.where(last, 0.0, v) for v in change(G, F, H, 7)]
        g = jnp.where(last, ini[:, lane], G[7])
        g7[:, lane] = g
        return [
            d0 + g,
            d1 + 6.0 * (d0 + g),
            d2 + 6.0 * d1 + 8.0 * d0 + 9.0 * g,
            6.0 * d2 + 8.0 * d1 + 4.0 * g,
            8.0 * d2,
        ]

    def second(lane):
        G, F, H = fields(lane)
        a0, a1, a2 = change(G, F, H, 3)
        b0, b1, b2 = change(G, F, H, 4)
        c0, c1, c2 = change(G, F, H, 5)
        e0, e1, e2 = change(G, F, H, 6)
        return [
            a0 + b0 + c0 + e0,
            a1 + 6.0 * a0 + b1 + 4.0 * b0 + c1 + 2.0 * c0 + e1,
            a2 + 6.0 * a1 + 8.0 * a0 + b2 + 4.0 * b1 + c2 + 2.0 * c1 + e2,
            6.0 * a2 + 8.0 * a1 + 4.0 * b2 + 2.0 * c2,
            8.0 * a2,
        ]

    def third(lane):
        G, F, H = fields(lane)
        b1 = F[0]
        b0 = b1 + H[0] - G[0]
        c0, c1, c2 = change(G, F, H, 1)
        e0, e1, e2 = change(G, F, H, 2)
        return [
            b0 + c0 + e0,
            b1 + 4.0 * b0 + c1 + 2.0 * c0 + e1,
            4.0 * b1 + c2 + 2.0 * c1 + e2,
            2.0 * c2,
        ]

    def combine(p, make):
        def one(j, carry):
            lane = pl.ds(pl.multiple_of(j * 128, 128), 128)
            for m, v in enumerate(add_squares(make(lane))):
                px[p, m, own, lane] = v
            return carry

        lax.fori_loop(0, cols // 128, one, 0)

    def power(p, m, side):
        h = m
        if side == 0:
            src, dst, dev = pl.ds(16 - h, h), pl.ds(8 - h, h), (tm, xs[0])
        else:
            src, dst, dev = pl.ds(8, h), pl.ds(16, h), (tm, xs[1])
        return pltpu.make_async_remote_copy(
            src_ref=px.at[p, m, src],
            dst_ref=px.at[p, m, dst],
            send_sem=es.at[p, m - 1, side],
            recv_sem=er.at[p, m - 1, side],
            device_id=dev,
            device_id_type=MESH,
        )

    def send_powers(p, top):
        for m in range(top, 0, -1):
            for side in (0, 1):
                power(p, m, side).start()

    combine(0, first)
    pl.semaphore_wait(barrier, len(peers))

    coef = halo(cx, (slice(None),), 5)
    send_powers(0, DEPTH)
    combine(1, second)
    send_powers(1, DEPTH)
    combine(2, third)
    px[2, DEPTH] = jnp.zeros_like(px[2, DEPTH])
    send_powers(2, DEPTH - 1)
    early = halo(gx, (pl.ds(1, 7),), 2) + halo(fx, (slice(None),), 1) + onward(g7, gx, (0,), 2)

    for cp in coef:
        cp.wait_recv()

    def weights(t, carry):
        rows = pl.ds(pl.multiple_of(t * 8, 8), 8)
        dif, vx, vy, rea = cx[0, rows], cx[1, rows], cx[2, rows], cx[3, rows]
        row = lax.broadcasted_iota(jnp.int32, dif.shape, 0) + t * 8
        col = lax.broadcasted_iota(jnp.int32, dif.shape, 1)
        top = (row == PAD) & (sx == 0)
        bottom = (row == PAD + 7) & (sx == strips - 1)
        wx[0, rows] = jnp.where(col == 0, 0.0, dif + jnp.maximum(vx, 0.0))
        wx[1, rows] = jnp.where(col == cols - 1, 0.0, dif - jnp.minimum(vx, 0.0))
        wx[2, rows] = jnp.where(top, 0.0, dif + jnp.maximum(vy, 0.0))
        wx[3, rows] = jnp.where(bottom, 0.0, dif - jnp.minimum(vy, 0.0))
        wx[4, rows] = -(4.0 * dif + jnp.abs(vx) + jnp.abs(vy) + rea)
        decx[rows] = jnp.exp(-8.0 * rea)
        return carry

    lax.fori_loop(0, 3, weights, 0)

    def ap(v):
        n = v.shape[0]
        return (
            wx[4] * v
            + wx[0] * pltpu.roll(v, 1, 1)
            + wx[1] * pltpu.roll(v, cols - 1, 1)
            + wx[2] * pltpu.roll(v, 1, 0)
            + wx[3] * pltpu.roll(v, n - 1, 0)
        )

    def mid(v):
        return v[PAD : PAD + 8]

    def horner(p, carry):
        @pl.when(p < 2)
        def _():
            for side in (0, 1):
                power(p, DEPTH, side).wait_recv()

        for m in range(DEPTH - 1, 0, -1):
            for side in (0, 1):
                power(p, m, side).wait_recv()

        def level(i, v):
            return ap(v) + px[p, DEPTH - 1 - i]

        v = lax.fori_loop(0, DEPTH, level, px[p, DEPTH])
        rx[p, own] = mid(v)
        return carry

    lax.fori_loop(0, 3, horner, 0)

    dec = decx[own]
    first_value = rx[0, own]
    part = jnp.where(last, first_value, dec * (dec * rx[2, own] + rx[1, own]) + first_value)
    for h in (0, 1):
        for j in range(8):
            sp[8 * h + j] = part[4 * h : 4 * h + 4, 128 * j : 128 * j + 128]
            dp[8 * h + j] = dec[4 * h : 4 * h + 4, 128 * j : 128 * j + 128]

    scatter = []
    for m in range(1, GROUP):
        to = lax.rem(q + m, GROUP)
        scatter.append(send(sp.at[to], r1.at[q], (y * GROUP + to, sx)))
    r1[q] = sp[q]
    d1 = dp[q]
    d2 = d1 * d1

    for cp in early:
        cp.wait_recv()

    def changes(k, carry):
        g, f = gx[k], fx[k]
        v = ap(g) + 2.0 * g + f
        dx[k + 1, own] = mid(ap(v)) + mid(g + f) + hx[k] - gx[k + 1, own]
        return carry

    lax.fori_loop(0, 8, changes, 0)
    d7[...] = jnp.where(last, 0.0, dx[8, own])
    middle = []
    for k, h in ((0, 3), (1, 2), (3, 4), (4, 3), (5, 2)):
        middle += halo(dx, (k + 1,), h)
    middle += onward(d7, dx, (0,), 4)
    late = halo(rx, (2,), 3) + onward(rx.at[0, own], tx, (), 3)

    for cp in scatter:
        cp.wait_recv()
    acc = jnp.zeros_like(d2)
    fac = jnp.ones_like(d2)
    for i in range(GROUP):
        pre[i] = acc
        pw[i] = fac
        acc = d2 * acc + r1[i]
        fac = d2 * fac
    r2[y] = jnp.where(y == slabs - 1, r1[GROUP - 1], acc)
    across = []
    for m in range(1, slabs):
        to = lax.rem(y + m, slabs)
        across.append(send(r2.at[y], r2.at[y], (to * GROUP + q, sx)))

    for cp in middle:
        cp.wait_recv()
    zx[0] = gx[0] + dx[0]

    def twice(v):
        v = v + ap(v)
        return mid(v) + mid(ap(v))

    def blocks(b, carry):
        k = 4 * b
        a = dx[k]
        bb = dx[k + 1]
        c = dx[k + 2]
        zx[k + 1, own] = gx[k + 1, own] + mid(bb) + twice(a)
        w = a + 2.0 * ap(a) + bb
        zx[k + 2, own] = gx[k + 2, own] + mid(c) + twice(w)
        w = w + 2.0 * ap(w) + c
        zx[k + 3, own] = gx[k + 3, own] + dx[k + 3, own] + twice(w)
        zx[k + 4, own] = gx[k + 4, own] + dx[k + 4, own]
        return carry

    lax.fori_loop(0, 2, blocks, 0)
    coarse = halo(zx, (pl.ds(1, 7),), 1)

    for cp in across:
        cp.wait_recv()
    acc = r2[slabs - 1]
    for i in range(slabs - 1):
        acc = jnp.where(i < y, fac * acc + r2[i], acc)
    for i in range(GROUP):
        wo[i] = pw[i] * acc + pre[i]
    half = q // 8
    tile = lax.rem(q, 8)
    side = lax.rem(sx + 2 * half + strips - 1, strips)
    gather = []
    for m in range(GROUP):
        to = lax.rem(q + m, GROUP)
        dev = y * GROUP + to
        if m:
            gather.append(send(wo.at[to], ce.at[tile, 1 + half], (dev, sx)))
        gather.append(send(wo.at[to], ce.at[tile, 3 - 3 * half], (dev, side)))
    ce[tile, 1 + half] = wo[q]

    for cp in coarse:
        cp.wait_recv()

    def results(k, carry):
        v = zx[k]
        ob[2 * k] = mid(v) + mid(ap(v)) + fx[k, own]
        ob[2 * k + 1] = zx[k + 1, own]
        return carry

    lax.fori_loop(0, 8, results, 0)
    for cp in late:
        cp.wait_recv()

    for cp in gather:
        cp.wait_recv()
    for j in range(8):
        lane = pl.ds(128 * j, 128)
        for quarter in range(4):
            cex[pl.ds(4 + 4 * quarter, 4), lane] = ce[j, quarter]
    v = cex[...]
    w = v + rx[2]
    ex[0] = (v - tx[...]) * jnp.exp(8.0 * cx[3])
    ex[1] = w
    ex[2, own] = mid(decx[...] * w) + rx[1, own]
    stores = []

    def finish(b, carry):
        e = ex[b]
        a1 = ap(e)
        a2 = ap(a1)
        a3 = mid(ap(a2))
        e, a1, a2 = mid(e), mid(a1), mid(a2)
        k = 8 * b
        ob[k] += e + a1
        ob[k + 1] += e + 2.0 * a1
        ob[k + 2] += e + 3.0 * a1 + 2.0 * a2
        ob[k + 3] += e + 4.0 * a1
        ob[k + 4] += e + 5.0 * a1 + 4.0 * a2
        ob[k + 5] += e + 6.0 * a1 + 8.0 * a2
        ob[k + 6] += e + 7.0 * a1 + 14.0 * a2 + 8.0 * a3
        ob[k + 7] += ex[b + 1, own]
        pltpu.make_async_copy(ob.at[pl.ds(k, 8)], out.at[pl.ds(k, 8)], lsem.at[b]).start()
        return carry

    lax.fori_loop(0, 2, finish, 0)
    for b in range(2):
        pltpu.make_async_copy(ob.at[pl.ds(8 * b, 8)], out.at[pl.ds(8 * b, 8)], lsem.at[b]).wait()
    for cp in sent:
        cp.wait_send()
    for p in range(3):
        for m in range(1, DEPTH + 1 - p // 2):
            for s in (0, 1):
                power(p, m, s).wait_send()


def body(slabs, strips, u_coarse_guess, forcing, u_init, diffuse, vel_x, vel_y, react):
    points, rows, cols = u_coarse_guess.shape
    wide = rows + 2 * PAD
    copies = 2 + 4 + 3 + 15 + 10 + 3 + 2 + 3 + 7 + 2 + 31
    f32 = jnp.float32

    def vmem(*shape):
        return pltpu.VMEM(shape, f32)

    return pl.pallas_call(
        functools.partial(kernel, slabs, strips),
        out_shape=jax.ShapeDtypeStruct(forcing.shape, f32),
        in_specs=[pl.BlockSpec(memory_space=pl.ANY)] * 7,
        out_specs=pl.BlockSpec(memory_space=pl.ANY),
        scratch_shapes=[
            vmem(points + 1, wide, cols),
            vmem(points, wide, cols),
            vmem(points, rows, cols),
            vmem(4, wide, cols),
            vmem(5, wide, cols),
            vmem(wide, cols),
            vmem(3, DEPTH + 1, wide, cols),
            vmem(points + 1, wide, cols),
            vmem(points + 1, wide, cols),
            vmem(3, wide, cols),
            vmem(wide, cols),
            vmem(3, wide, cols),
            vmem(2 * points, rows, cols),
            vmem(rows, cols),
            vmem(rows, cols),
            vmem(rows, cols),
            vmem(GROUP, 4, 128),
            vmem(GROUP, 4, 128),
            vmem(GROUP, 4, 128),
            vmem(GROUP, 4, 128),
            vmem(GROUP, 4, 128),
            vmem(slabs, 4, 128),
            vmem(GROUP, 4, 128),
            vmem(8, 4, 4, 128),
            vmem(wide, cols),
            pltpu.SemaphoreType.DMA((8,)),
            pltpu.SemaphoreType.DMA((3, DEPTH, 2)),
            pltpu.SemaphoreType.DMA((3, DEPTH, 2)),
            pltpu.SemaphoreType.DMA((copies,)),
            pltpu.SemaphoreType.DMA((copies,)),
        ],
        compiler_params=pltpu.CompilerParams(
            collective_id=0, has_side_effects=True, vmem_limit_bytes=32 << 20
        ),
        cost_estimate=pl.CostEstimate(flops=10_000_000, bytes_accessed=1_500_000, transcendentals=16384),
    )(
        u_coarse_guess,
        forcing.reshape(points, 2, rows, cols),
        u_init,
        diffuse,
        vel_x,
        vel_y,
        react,
    )


def solution(mesh):
    slabs = mesh.shape["tm"] // GROUP
    strips = mesh.shape["space"]
    whole = P("tm", "space", None)
    row = P("space", None)
    return jax.shard_map(
        functools.partial(body, slabs, strips),
        mesh=mesh,
        in_specs=(whole, whole) + (row,) * 5,
        out_specs=whole,
        check_vma=False,
    )
```

profile of v0, /device:TPU:1, one launch (start us, length us, event | category | flops | bytes accessed | tf_op | source)
XLA Modules:
  0.0 52.1 jit_solution(15479379712811574303)
XLA Ops:
  0.0 0.0 copy-start
  0.0 1.0 %copy-done = f32[16,8,1024]{2,1,0:T(8,128)S(1)} copy-done((f32[16,8,1024]{2,1,0:T(8,128)S(1)}, f32[16,8,1024]{2,1,0:T(8,128)}, u32[]{:S(2)}) %copy-start) | copy-done | bytes 524312
  1.0 0.0 copy-start.1
  1.0 0.9 %copy-done.1 = f32[8,8,1024]{2,1,0:T(8,128)S(1)} copy-done((f32[8,8,1024]{2,1,0:T(8,128)S(1)}, f32[8,8,1024]{2,1,0:T(8,128)}, u32[]{:S(2)}) %copy-start.1) | copy-done | bytes 262168
  2.0 0.0 copy-start.2
  2.0 0.8 %copy-done.2 = f32[8,1024]{1,0:T(8,128)S(1)} copy-done((f32[8,1024]{1,0:T(8,128)S(1)}, f32[8,1024]{1,0:T(8,128)}, u32[]{:S(2)}) %copy-start.2) | copy-done | bytes 32792
  2.8 0.0 copy-start.3
  2.8 0.8 %copy-done.3 = f32[8,1024]{1,0:T(8,128)S(1)} copy-done((f32[8,1024]{1,0:T(8,128)S(1)}, f32[8,1024]{1,0:T(8,128)}, u32[]{:S(2)}) %copy-start.3) | copy-done | bytes 32792
  3.5 0.0 copy-start.4
  3.5 0.8 %copy-done.4 = f32[8,1024]{1,0:T(8,128)S(1)} copy-done((f32[8,1024]{1,0:T(8,128)S(1)}, f32[8,1024]{1,0:T(8,128)}, u32[]{:S(2)}) %copy-start.4) | copy-done | bytes 32792
  4.3 0.0 copy-start.5
  4.3 0.8 %copy-done.5 = f32[8,1024]{1,0:T(8,128)S(1)} copy-done((f32[8,1024]{1,0:T(8,128)S(1)}, f32[8,1024]{1,0:T(8,128)}, u32[]{:S(2)}) %copy-start.5) | copy-done | bytes 32792
  5.0 0.0 copy-start.6
  5.0 0.8 %copy-done.6 = f32[8,1024]{1,0:T(8,128)S(1)} copy-done((f32[8,1024]{1,0:T(8,128)S(1)}, f32[8,1024]{1,0:T(8,128)}, u32[]{:S(2)}) %copy-start.6) | copy-done | bytes 32792
  5.8 45.6 %shard_map.73 = f32[16,8,1024]{2,1,0:T(8,128)S(1)} custom-call(f32[8,8,1024]{2,1,0:T(8,128)S(1)} %copy-done.1, f32[8,2,8,1024]{3,2,1,0:T(8,128)S(1)} %bitcast.1, f32[8,1024]{1,0:T(8,128)S(1)} %copy-done.2, f32[8,1024]{1,0:T(8,128)S(1)} %copy-done.3, f32[8,1024]{1,0:T(8,128)S(1)} %copy-done.4, f32[8,1024]{1,0:T(8,128)S(1)} %copy-done.5, f32[8,1024]{1,0:T(8,128)S(1)} %copy-done.6), custom_call_target="tpu_custom_call" | custom-call | flops 10000000 | bytes 1500000 | tf_op jit(solution)/shard_map/pallas_call | solution.py:456
  51.3 0.8 %copy.9 = f32[16,8,1024]{2,1,0:T(8,128)} copy(f32[16,8,1024]{2,1,0:T(8,128)S(1)} %shard_map.73) | data formatting | bytes 1048576
Async XLA Ops:
  0.0 1.0 %copy-start = (f32[16,8,1024]{2,1,0:T(8,128)S(1)}, f32[16,8,1024]{2,1,0:T(8,128)}, u32[]{:S(2)}) copy-start(f32[16,8,1024]{2,1,0:T(8,128)} %param.8) | copy-start | bytes 1572868
  1.0 0.9 %copy-start.1 = (f32[8,8,1024]{2,1,0:T(8,128)S(1)}, f32[8,8,1024]{2,1,0:T(8,128)}, u32[]{:S(2)}) copy-start(f32[8,8,1024]{2,1,0:T(8,128)} %guess.1) | copy-start | bytes 786436
  2.0 0.8 %copy-start.2 = (f32[8,1024]{1,0:T(8,128)S(1)}, f32[8,1024]{1,0:T(8,128)}, u32[]{:S(2)}) copy-start(f32[8,1024]{1,0:T(8,128)} %init.1) | copy-start | bytes 98308
  2.8 0.8 %copy-start.3 = (f32[8,1024]{1,0:T(8,128)S(1)}, f32[8,1024]{1,0:T(8,128)}, u32[]{:S(2)}) copy-start(f32[8,1024]{1,0:T(8,128)} %diffuse.1) | copy-start | bytes 98308
  3.5 0.8 %copy-start.4 = (f32[8,1024]{1,0:T(8,128)S(1)}, f32[8,1024]{1,0:T(8,128)}, u32[]{:S(2)}) copy-start(f32[8,1024]{1,0:T(8,128)} %vel_x.1) | copy-start | bytes 98308
  4.3 0.8 %copy-start.5 = (f32[8,1024]{1,0:T(8,128)S(1)}, f32[8,1024]{1,0:T(8,128)}, u32[]{:S(2)}) copy-start(f32[8,1024]{1,0:T(8,128)} %vel_y.1) | copy-start | bytes 98308
  5.0 0.8 %copy-start.6 = (f32[8,1024]{1,0:T(8,128)S(1)}, f32[8,1024]{1,0:T(8,128)}, u32[]{:S(2)}) copy-start(f32[8,1024]{1,0:T(8,128)} %react.1) | copy-start | bytes 98308
where the time goes:
time: 52.7 us; the launch traced here: 52.1 us
  Pallas kernels  45.6 us (87%)
  local copies, waits for them, and re-layouts  6.57 us (12%)
    pallas_call x1, Pallas kernels, body(): pl.pallas_call(functools.partial(kernel, slabs, strips), out_shape=jax.Sh...  45.6 us
    unnamed x15, local copies, waits for them, and re-layouts  6.57 us

commit v1 on v0

--- a/solution.py
+++ b/solution.py
@@ -14,7 +14,6 @@
 
 
 def add_squares(x):
-    zero = None
     out = []
     for m in range(len(x) + 2):
         terms = []
@@ -28,7 +27,6 @@
         for t in terms[1:]:
             total = total + t
         out.append(total)
-    del zero
     return out
 
 
@@ -53,6 +51,8 @@
     dx,
     zx,
     rx,
+    qx,
+    fp,
     tx,
     ex,
     ob,
@@ -67,10 +67,9 @@
     r2,
     wo,
     ce,
+    ch,
     cex,
     lsem,
-    es,
-    er,
     ss,
     sr,
 ):
@@ -135,6 +134,36 @@
         sent.append(cp)
         return cp
 
+    class Batch:
+        def __init__(self, items, whole):
+            i = slot[0]
+            slot[0] += 1
+            for src, dst, dev in items:
+                self.copy = pltpu.make_async_remote_copy(
+                    src_ref=src,
+                    dst_ref=dst,
+                    send_sem=ss.at[i],
+                    recv_sem=sr.at[i],
+                    device_id=dev,
+                    device_id_type=MESH,
+                )
+                self.copy.start()
+            self.total = pltpu.make_async_remote_copy(
+                src_ref=whole,
+                dst_ref=whole,
+                send_sem=ss.at[i],
+                recv_sem=sr.at[i],
+                device_id=items[0][2],
+                device_id_type=MESH,
+            )
+            sent.append(self.total)
+
+        def wait_recv(self):
+            self.total.wait_recv()
+
+    def far_first(n):
+        return sorted(range(1, n), key=lambda m: -min(m, n - m))
+
     def halo(ref, lead, h):
         a = send(ref.at[lead + (pl.ds(16 - h, h),)], ref.at[lead + (pl.ds(8 - h, h),)], (tm, xs[0]))
         b = send(ref.at[lead + (pl.ds(8, h),)], ref.at[lead + (pl.ds(16, h),)], (tm, xs[1]))
@@ -209,42 +238,18 @@
         def one(j, carry):
             lane = pl.ds(pl.multiple_of(j * 128, 128), 128)
             for m, v in enumerate(add_squares(make(lane))):
-                px[p, m, own, lane] = v
+                px[p, m, :, lane] = v
             return carry
 
         lax.fori_loop(0, cols // 128, one, 0)
 
-    def power(p, m, side):
-        h = m
-        if side == 0:
-            src, dst, dev = pl.ds(16 - h, h), pl.ds(8 - h, h), (tm, xs[0])
-        else:
-            src, dst, dev = pl.ds(8, h), pl.ds(16, h), (tm, xs[1])
-        return pltpu.make_async_remote_copy(
-            src_ref=px.at[p, m, src],
-            dst_ref=px.at[p, m, dst],
-            send_sem=es.at[p, m - 1, side],
-            recv_sem=er.at[p, m - 1, side],
-            device_id=dev,
-            device_id_type=MESH,
-        )
-
-    def send_powers(p, top):
-        for m in range(top, 0, -1):
-            for side in (0, 1):
-                power(p, m, side).start()
-
+    pl.semaphore_wait(barrier, len(peers))
+    coef = halo(cx, (slice(None),), DEPTH)
+    early = halo(gx, (pl.ds(1, 7),), 2) + halo(fx, (slice(None),), 1)
     combine(0, first)
-    pl.semaphore_wait(barrier, len(peers))
-
-    coef = halo(cx, (slice(None),), 5)
-    send_powers(0, DEPTH)
+    early += onward(g7, gx, (0,), 2)
     combine(1, second)
-    send_powers(1, DEPTH)
     combine(2, third)
-    px[2, DEPTH] = jnp.zeros_like(px[2, DEPTH])
-    send_powers(2, DEPTH - 1)
-    early = halo(gx, (pl.ds(1, 7),), 2) + halo(fx, (slice(None),), 1) + onward(g7, gx, (0,), 2)
 
     for cp in coef:
         cp.wait_recv()
@@ -254,14 +259,19 @@
         dif, vx, vy, rea = cx[0, rows], cx[1, rows], cx[2, rows], cx[3, rows]
         row = lax.broadcasted_iota(jnp.int32, dif.shape, 0) + t * 8
         col = lax.broadcasted_iota(jnp.int32, dif.shape, 1)
+        inside = (row >= PAD - DEPTH) & (row < PAD + 8 + DEPTH)
+        inside &= (row >= PAD) | (sx > 0)
+        inside &= (row < PAD + 8) | (sx < strips - 1)
         top = (row == PAD) & (sx == 0)
         bottom = (row == PAD + 7) & (sx == strips - 1)
-        wx[0, rows] = jnp.where(col == 0, 0.0, dif + jnp.maximum(vx, 0.0))
-        wx[1, rows] = jnp.where(col == cols - 1, 0.0, dif - jnp.minimum(vx, 0.0))
-        wx[2, rows] = jnp.where(top, 0.0, dif + jnp.maximum(vy, 0.0))
-        wx[3, rows] = jnp.where(bottom, 0.0, dif - jnp.minimum(vy, 0.0))
-        wx[4, rows] = -(4.0 * dif + jnp.abs(vx) + jnp.abs(vy) + rea)
-        decx[rows] = jnp.exp(-8.0 * rea)
+        west = jnp.where(col == 0, 0.0, dif + jnp.maximum(vx, 0.0))
+        east = jnp.where(col == cols - 1, 0.0, dif - jnp.minimum(vx, 0.0))
+        north = jnp.where(top, 0.0, dif + jnp.maximum(vy, 0.0))
+        south = jnp.where(bottom, 0.0, dif - jnp.minimum(vy, 0.0))
+        centre = -(4.0 * dif + jnp.abs(vx) + jnp.abs(vy) + rea)
+        for i, v in enumerate((west, east, north, south, centre)):
+            wx[i, rows] = jnp.where(inside, v, 0.0)
+        decx[rows] = jnp.where(inside, jnp.exp(-8.0 * rea), 0.0)
         return carry
 
     lax.fori_loop(0, 3, weights, 0)
@@ -279,38 +289,49 @@
     def mid(v):
         return v[PAD : PAD + 8]
 
+    def around(v):
+        none = jnp.zeros_like(v)
+        return jnp.concatenate([none, v, none], axis=0)
+
     def horner(p, carry):
-        @pl.when(p < 2)
-        def _():
-            for side in (0, 1):
-                power(p, DEPTH, side).wait_recv()
-
-        for m in range(DEPTH - 1, 0, -1):
-            for side in (0, 1):
-                power(p, m, side).wait_recv()
+        top = DEPTH - p // 2
 
         def level(i, v):
-            return ap(v) + px[p, DEPTH - 1 - i]
-
-        v = lax.fori_loop(0, DEPTH, level, px[p, DEPTH])
-        rx[p, own] = mid(v)
+            return ap(v) + around(px[p, top - 1 - i])
+
+        rx[p] = lax.fori_loop(0, top, level, around(px[p, top]))
         return carry
 
     lax.fori_loop(0, 3, horner, 0)
 
-    dec = decx[own]
-    first_value = rx[0, own]
-    part = jnp.where(last, first_value, dec * (dec * rx[2, own] + rx[1, own]) + first_value)
+    decv = decx[...]
+    dec = mid(decv)
+    value = rx[0]
+    part = jnp.where(last, value, decv * (decv * rx[2] + rx[1]) + value)
     for h in (0, 1):
         for j in range(8):
-            sp[8 * h + j] = part[4 * h : 4 * h + 4, 128 * j : 128 * j + 128]
             dp[8 * h + j] = dec[4 * h : 4 * h + 4, 128 * j : 128 * j + 128]
-
-    scatter = []
-    for m in range(1, GROUP):
+            for t in range(3):
+                r = 8 * t + 4 * h
+                sp[t, 8 * h + j] = part[r : r + 4, 128 * j : 128 * j + 128]
+
+    def mate(m):
         to = lax.rem(q + m, GROUP)
-        scatter.append(send(sp.at[to], r1.at[q], (y * GROUP + to, sx)))
-    r1[q] = sp[q]
+        return to, y * GROUP + to
+
+    items = ([], [], [])
+    for m in far_first(GROUP) + [0]:
+        to, dev = mate(m)
+        items[2].append((sp.at[2, to], r1.at[2, q], (dev, xs[0])))
+        items[0].append((sp.at[0, to], r1.at[0, q], (dev, xs[1])))
+        if m:
+            items[1].append((sp.at[1, to], r1.at[1, q], (dev, sx)))
+    scatter = [Batch(items[2], r1.at[2]), Batch(items[0], r1.at[0]), Batch(items[1], r1.at[1, pl.ds(0, GROUP - 1)])]
+    r1[1, q] = sp[1, q]
+    spill = [
+        send(rx.at[:, pl.ds(16, DEPTH)], qx.at[0, :, pl.ds(0, DEPTH)], (tm, xs[0])),
+        send(rx.at[:, pl.ds(8 - DEPTH, DEPTH)], qx.at[1, :, pl.ds(8 - DEPTH, DEPTH)], (tm, xs[1])),
+    ]
     d1 = dp[q]
     d2 = d1 * d1
 
@@ -329,7 +350,14 @@
     for k, h in ((0, 3), (1, 2), (3, 4), (4, 3), (5, 2)):
         middle += halo(dx, (k + 1,), h)
     middle += onward(d7, dx, (0,), 4)
-    late = halo(rx, (2,), 3) + onward(rx.at[0, own], tx, (), 3)
+    for cp in spill:
+        cp.wait_recv()
+    row = lax.broadcasted_iota(jnp.int32, (8, cols), 0)
+    for p in range(3):
+        above = jnp.where(row < DEPTH, qx[0, p], 0.0)
+        below = jnp.where(row >= 8 - DEPTH, qx[1, p], 0.0)
+        fp[p, own] = rx[p, own] + above + below
+    late = halo(fp, (2,), 3) + onward(fp.at[0, own], tx, (), 3)
 
     for cp in scatter:
         cp.wait_recv()
@@ -338,13 +366,14 @@
     for i in range(GROUP):
         pre[i] = acc
         pw[i] = fac
-        acc = d2 * acc + r1[i]
+        part = r1[1, i] + r1[2, i] + r1[0, i]
+        acc = d2 * acc + part
         fac = d2 * fac
-    r2[y] = jnp.where(y == slabs - 1, r1[GROUP - 1], acc)
-    across = []
-    for m in range(1, slabs):
-        to = lax.rem(y + m, slabs)
-        across.append(send(r2.at[y], r2.at[y], (to * GROUP + q, sx)))
+    r2[y] = jnp.where(y == slabs - 1, part, acc)
+    items = []
+    for m in far_first(slabs):
+        items.append((r2.at[y], r2.at[y], (lax.rem(y + m, slabs) * GROUP + q, sx)))
+    across = [Batch(items, r2.at[pl.ds(0, slabs - 1)])]
 
     for cp in middle:
         cp.wait_recv()
@@ -378,16 +407,16 @@
     for i in range(GROUP):
         wo[i] = pw[i] * acc + pre[i]
     half = q // 8
-    tile = lax.rem(q, 8)
     side = lax.rem(sx + 2 * half + strips - 1, strips)
-    gather = []
-    for m in range(GROUP):
-        to = lax.rem(q + m, GROUP)
-        dev = y * GROUP + to
+    items = ([], [])
+    for m in far_first(GROUP) + [0]:
+        to, dev = mate(m)
+        items[0].append((wo.at[to], ch.at[q], (dev, side)))
         if m:
-            gather.append(send(wo.at[to], ce.at[tile, 1 + half], (dev, sx)))
-        gather.append(send(wo.at[to], ce.at[tile, 3 - 3 * half], (dev, side)))
-    ce[tile, 1 + half] = wo[q]
+            items[1].append((wo.at[to], ce.at[q], (dev, sx)))
+    early_sent = list(sent)
+    gather = [Batch(items[0], ch), Batch(items[1], ce.at[pl.ds(0, GROUP - 1)])]
+    ce[q] = wo[q]
 
     for cp in coarse:
         cp.wait_recv()
@@ -401,18 +430,22 @@
     lax.fori_loop(0, 8, results, 0)
     for cp in late:
         cp.wait_recv()
+    for cp in early_sent:
+        cp.wait_send()
 
     for cp in gather:
         cp.wait_recv()
     for j in range(8):
         lane = pl.ds(128 * j, 128)
-        for quarter in range(4):
-            cex[pl.ds(4 + 4 * quarter, 4), lane] = ce[j, quarter]
+        cex[4:8, lane] = ch[8 + j]
+        cex[8:12, lane] = ce[j]
+        cex[12:16, lane] = ce[8 + j]
+        cex[16:20, lane] = ch[j]
     v = cex[...]
-    w = v + rx[2]
+    w = v + fp[2]
     ex[0] = (v - tx[...]) * jnp.exp(8.0 * cx[3])
     ex[1] = w
-    ex[2, own] = mid(decx[...] * w) + rx[1, own]
+    ex[2, own] = mid(decx[...] * w) + fp[1, own]
     stores = []
 
     def finish(b, carry):
@@ -436,18 +469,14 @@
     lax.fori_loop(0, 2, finish, 0)
     for b in range(2):
         pltpu.make_async_copy(ob.at[pl.ds(8 * b, 8)], out.at[pl.ds(8 * b, 8)], lsem.at[b]).wait()
-    for cp in sent:
-        cp.wait_send()
-    for p in range(3):
-        for m in range(1, DEPTH + 1 - p // 2):
-            for s in (0, 1):
-                power(p, m, s).wait_send()
+    for cp in gather:
+        cp.total.wait_send()
 
 
 def body(slabs, strips, u_coarse_guess, forcing, u_init, diffuse, vel_x, vel_y, react):
     points, rows, cols = u_coarse_guess.shape
     wide = rows + 2 * PAD
-    copies = 2 + 4 + 3 + 15 + 10 + 3 + 2 + 3 + 7 + 2 + 31
+    copies = 2 + 4 + 3 + 3 + 2 + 10 + 3 + 2 + 3 + 1 + 2 + 2
     f32 = jnp.float32
 
     def vmem(*shape):
@@ -456,7 +485,7 @@
     return pl.pallas_call(
         functools.partial(kernel, slabs, strips),
         out_shape=jax.ShapeDtypeStruct(forcing.shape, f32),
-        in_specs=[pl.BlockSpec(memory_space=pl.ANY)] * 7,
+        in_specs=[pl.BlockSpec(memory_space=pltpu.HBM)] * 7,
         out_specs=pl.BlockSpec(memory_space=pl.ANY),
         scratch_shapes=[
             vmem(points + 1, wide, cols),
@@ -465,9 +494,11 @@
             vmem(4, wide, cols),
             vmem(5, wide, cols),
             vmem(wide, cols),
-            vmem(3, DEPTH + 1, wide, cols),
+            vmem(3, DEPTH + 1, rows, cols),
             vmem(points + 1, wide, cols),
             vmem(points + 1, wide, cols),
+            vmem(3, wide, cols),
+            vmem(2, 3, rows, cols),
             vmem(3, wide, cols),
             vmem(wide, cols),
             vmem(3, wide, cols),
@@ -475,23 +506,22 @@
             vmem(rows, cols),
             vmem(rows, cols),
             vmem(rows, cols),
+            vmem(3, GROUP, 4, 128),
             vmem(GROUP, 4, 128),
-            vmem(GROUP, 4, 128),
-            vmem(GROUP, 4, 128),
+            vmem(3, GROUP, 4, 128),
             vmem(GROUP, 4, 128),
             vmem(GROUP, 4, 128),
             vmem(slabs, 4, 128),
             vmem(GROUP, 4, 128),
-            vmem(8, 4, 4, 128),
+            vmem(GROUP, 4, 128),
+            vmem(GROUP, 4, 128),
             vmem(wide, cols),
             pltpu.SemaphoreType.DMA((8,)),
-            pltpu.SemaphoreType.DMA((3, DEPTH, 2)),
-            pltpu.SemaphoreType.DMA((3, DEPTH, 2)),
             pltpu.SemaphoreType.DMA((copies,)),
             pltpu.SemaphoreType.DMA((copies,)),
         ],
         compiler_params=pltpu.CompilerParams(
-            collective_id=0, has_side_effects=True, vmem_limit_bytes=32 << 20
+            collective_id=0, has_side_effects=True, vmem_limit_bytes=60 << 20
         ),
         cost_estimate=pl.CostEstimate(flops=10_000_000, bytes_accessed=1_500_000, transcendentals=16384),
     )(

time: 52.7 us -> 44 us (0.83)
  local copies, waits for them, and re-layouts: 6.57 us -> 1.89 us
  Pallas kernels: 45.6 us -> 41.9 us
    unnamed x15 -> x1, local copies, waits for them, and re-layouts: 6.57 us -> 1.89 us
    pallas_call x1, Pallas kernels: 45.6 us -> 41.9 us  [body(): pl.pallas_call(functools.partial(kernel, slabs, strips), out_shape=jax.Sh...]
where the time goes in v1:
time: 44 us; the launch traced here: 43.8 us
  Pallas kernels  41.9 us (95%)
  local copies, waits for them, and re-layouts  1.89 us (4%)
    pallas_call x1, Pallas kernels, body(): pl.pallas_call(functools.partial(kernel, slabs, strips), out_shape=jax.Sh...  41.9 us
    unnamed x1, local copies, waits for them, and re-layouts  1.89 us

profile of v1, /device:TPU:1, one launch (start us, length us, event | category | flops | bytes accessed | tf_op | source)
XLA Modules:
  0.0 43.8 jit_solution(17834052135653171736)
XLA Ops:
  0.0 41.9 %shard_map.73 = f32[16,8,1024]{2,1,0:T(8,128)} custom-call(f32[8,8,1024]{2,1,0:T(8,128)} %guess.1, f32[8,2,8,1024]{3,2,1,0:T(8,128)} %bitcast.1, f32[8,1024]{1,0:T(8,128)} %init.1, f32[8,1024]{1,0:T(8,128)} %diffuse.1, f32[8,1024]{1,0:T(8,128)} %vel_x.1, f32[8,1024]{1,0:T(8,128)} %vel_y.1, f32[8,1024]{1,0:T(8,128)} %react.1), custom_call_target="tpu_custom_call" | custom-call | flops 10000000 | bytes 1500000 | tf_op jit(solution)/shard_map/pallas_call | solution.py:485
  41.9 1.9 %copy.9 = f32[16,8,1024]{2,1,0:T(8,128)} copy(f32[16,8,1024]{2,1,0:T(8,128)} %shard_map.73) | data formatting | bytes 1048576

commit v2 on v1

--- a/solution.py
+++ b/solution.py
@@ -10,6 +10,7 @@
 MESH = pl.DeviceIdType.MESH
 GROUP = 16
 PAD = 8
+NEAR = 4
 DEPTH = 6
 
 
@@ -40,12 +41,17 @@
     vel_x,
     vel_y,
     react,
-    out,
+    ob,
     gx,
     fx,
     hx,
     cx,
+    cn,
+    cf,
     wx,
+    wn,
+    inv,
+    rn,
     decx,
     px,
     dx,
@@ -55,7 +61,6 @@
     fp,
     tx,
     ex,
-    ob,
     ini,
     g7,
     d7,
@@ -83,7 +88,8 @@
     prv = lax.rem(tm + count - 1, count)
     last = tm == count - 1
     cols = ob.shape[2]
-    own = pl.ds(PAD, 8)
+    own = pl.ds(0, 8)
+    centre_rows = pl.ds(PAD, 8)
 
     barrier = pltpu.get_barrier_semaphore()
     peers = [(tm, s) for s in xs]
@@ -104,10 +110,10 @@
             (force.at[:, 0], fx.at[:, own]),
             (force.at[:, 1], hx),
             (init, ini),
-            (diffuse, cx.at[0, own]),
-            (vel_x, cx.at[1, own]),
-            (vel_y, cx.at[2, own]),
-            (react, cx.at[3, own]),
+            (diffuse, cx.at[0]),
+            (vel_x, cx.at[1]),
+            (vel_y, cx.at[2]),
+            (react, cx.at[3]),
         ]
     ):
         cp = pltpu.make_async_copy(src, dst, lsem.at[i])
@@ -165,15 +171,15 @@
         return sorted(range(1, n), key=lambda m: -min(m, n - m))
 
     def halo(ref, lead, h):
-        a = send(ref.at[lead + (pl.ds(16 - h, h),)], ref.at[lead + (pl.ds(8 - h, h),)], (tm, xs[0]))
-        b = send(ref.at[lead + (pl.ds(8, h),)], ref.at[lead + (pl.ds(16, h),)], (tm, xs[1]))
+        a = send(ref.at[lead + (pl.ds(8 - h, h),)], ref.at[lead + (pl.ds(16 - h, h),)], (tm, xs[0]))
+        b = send(ref.at[lead + (pl.ds(0, h),)], ref.at[lead + (pl.ds(8, h),)], (tm, xs[1]))
         return [a, b]
 
     def onward(src, ref, lead, h):
         return [
             send(src, ref.at[lead + (own,)], (nxt, sx)),
-            send(src.at[pl.ds(8 - h, h)], ref.at[lead + (pl.ds(8 - h, h),)], (nxt, xs[0])),
-            send(src.at[pl.ds(0, h)], ref.at[lead + (pl.ds(16, h),)], (nxt, xs[1])),
+            send(src.at[pl.ds(8 - h, h)], ref.at[lead + (pl.ds(16 - h, h),)], (nxt, xs[0])),
+            send(src.at[pl.ds(0, h)], ref.at[lead + (pl.ds(8, h),)], (nxt, xs[1])),
         ]
 
     def change(G, F, H, k):
@@ -244,68 +250,111 @@
         lax.fori_loop(0, cols // 128, one, 0)
 
     pl.semaphore_wait(barrier, len(peers))
-    coef = halo(cx, (slice(None),), DEPTH)
+
+    def parameters(dst, up, down, n):
+        return [
+            send(cx.at[:, pl.ds(up, n)], dst.at[:, pl.ds(up, n)], (tm, xs[0])),
+            send(cx.at[:, pl.ds(down, n)], dst.at[:, pl.ds(down, n)], (tm, xs[1])),
+        ]
+
+    near = parameters(cn, 8 - NEAR, 0, NEAR)
+    far = parameters(cf, 8 - DEPTH, NEAR, DEPTH - NEAR)
     early = halo(gx, (pl.ds(1, 7),), 2) + halo(fx, (slice(None),), 1)
     combine(0, first)
     early += onward(g7, gx, (0,), 2)
     combine(1, second)
     combine(2, third)
 
-    for cp in coef:
-        cp.wait_recv()
-
-    def weights(t, carry):
-        rows = pl.ds(pl.multiple_of(t * 8, 8), 8)
-        dif, vx, vy, rea = cx[0, rows], cx[1, rows], cx[2, rows], cx[3, rows]
-        row = lax.broadcasted_iota(jnp.int32, dif.shape, 0) + t * 8
-        col = lax.broadcasted_iota(jnp.int32, dif.shape, 1)
-        inside = (row >= PAD - DEPTH) & (row < PAD + 8 + DEPTH)
-        inside &= (row >= PAD) | (sx > 0)
-        inside &= (row < PAD + 8) | (sx < strips - 1)
-        top = (row == PAD) & (sx == 0)
-        bottom = (row == PAD + 7) & (sx == strips - 1)
+    row = lax.broadcasted_iota(jnp.int32, (8, cols), 0)
+    col = lax.broadcasted_iota(jnp.int32, (8, cols), 1)
+    low = row < NEAR
+    above = sx > 0
+    beneath = sx < strips - 1
+
+    def weights(raw, inside, top, bottom):
+        dif, vx, vy, rea = raw
         west = jnp.where(col == 0, 0.0, dif + jnp.maximum(vx, 0.0))
         east = jnp.where(col == cols - 1, 0.0, dif - jnp.minimum(vx, 0.0))
-        north = jnp.where(top, 0.0, dif + jnp.maximum(vy, 0.0))
-        south = jnp.where(bottom, 0.0, dif - jnp.minimum(vy, 0.0))
+        north = dif + jnp.maximum(vy, 0.0)
+        south = dif - jnp.minimum(vy, 0.0)
         centre = -(4.0 * dif + jnp.abs(vx) + jnp.abs(vy) + rea)
-        for i, v in enumerate((west, east, north, south, centre)):
-            wx[i, rows] = jnp.where(inside, v, 0.0)
-        decx[rows] = jnp.where(inside, jnp.exp(-8.0 * rea), 0.0)
-        return carry
-
-    lax.fori_loop(0, 3, weights, 0)
-
-    def ap(v):
+        if inside is not None:
+            return [jnp.where(inside, v, 0.0) for v in (west, east, north, south, centre)]
+        return [west, east, jnp.where(top, 0.0, north), jnp.where(bottom, 0.0, south), centre]
+
+    raw = [cx[i] for i in range(4)]
+    edge = weights(raw, None, (row == 0) & (sx == 0), (row == 7) & (sx == strips - 1))
+    for i, v in enumerate(edge):
+        wx[i, 8:16] = v
+        wn[i, 0:8] = v
+    decx[8:16] = jnp.exp(-8.0 * raw[3])
+    inv[0:8] = jnp.exp(8.0 * raw[3])
+
+    for cp in near:
+        cp.wait_recv()
+    raw = [cn[i] for i in range(4)]
+    for i, v in enumerate(weights(raw, (low & beneath) | (~low & above), None, None)):
+        wn[i, 8:16] = v
+    inv[8:16] = jnp.exp(8.0 * raw[3])
+
+    def stencil(w, v):
         n = v.shape[0]
         return (
-            wx[4] * v
-            + wx[0] * pltpu.roll(v, 1, 1)
-            + wx[1] * pltpu.roll(v, cols - 1, 1)
-            + wx[2] * pltpu.roll(v, 1, 0)
-            + wx[3] * pltpu.roll(v, n - 1, 0)
+            w[4] * v
+            + w[0] * pltpu.roll(v, 1, 1)
+            + w[1] * pltpu.roll(v, cols - 1, 1)
+            + w[2] * pltpu.roll(v, 1, 0)
+            + w[3] * pltpu.roll(v, n - 1, 0)
         )
 
+    def ap(v):
+        return stencil(wn, v)
+
     def mid(v):
-        return v[PAD : PAD + 8]
+        return v[0:8]
 
     def around(v):
         none = jnp.zeros_like(v)
         return jnp.concatenate([none, v, none], axis=0)
 
-    def horner(p, carry):
+    def horner_near(p, carry):
         top = DEPTH - p // 2
 
+        def start(m):
+            v = px[p, m]
+            return jnp.concatenate([v, jnp.zeros_like(v)], axis=0)
+
         def level(i, v):
-            return ap(v) + around(px[p, top - 1 - i])
-
-        rx[p] = lax.fori_loop(0, top, level, around(px[p, top]))
+            return ap(v) + start(top - 1 - i)
+
+        rn[p] = lax.fori_loop(0, NEAR, level, start(top))
         return carry
 
-    lax.fori_loop(0, 3, horner, 0)
+    lax.fori_loop(0, 3, horner_near, 0)
+
+    for cp in far:
+        cp.wait_recv()
+    for t, inside in ((0, (row >= PAD - DEPTH) & above), (2, (row < DEPTH) & beneath)):
+        raw = [jnp.where(low, cn[i] if t else cf[i], cf[i] if t else cn[i]) for i in range(4)]
+        for i, v in enumerate(weights(raw, inside, None, None)):
+            wx[i, 8 * t : 8 * t + 8] = v
+        decx[8 * t : 8 * t + 8] = jnp.where(inside, jnp.exp(-8.0 * raw[3]), 0.0)
+
+    def horner_far(p, carry):
+        top = DEPTH - p // 2
+
+        def level(i, v):
+            return stencil(wx, v) + around(px[p, top - 1 - NEAR - i])
+
+        v = rn[p, 8:16]
+        v = jnp.concatenate([jnp.where(low, 0.0, v), rn[p, 0:8], jnp.where(low, v, 0.0)], axis=0)
+        rx[p] = lax.fori_loop(0, top - NEAR, level, v)
+        return carry
+
+    lax.fori_loop(0, 3, horner_far, 0)
 
     decv = decx[...]
-    dec = mid(decv)
+    dec = decv[8:16]
     value = rx[0]
     part = jnp.where(last, value, decv * (decv * rx[2] + rx[1]) + value)
     for h in (0, 1):
@@ -352,11 +401,10 @@
     middle += onward(d7, dx, (0,), 4)
     for cp in spill:
         cp.wait_recv()
-    row = lax.broadcasted_iota(jnp.int32, (8, cols), 0)
     for p in range(3):
-        above = jnp.where(row < DEPTH, qx[0, p], 0.0)
-        below = jnp.where(row >= 8 - DEPTH, qx[1, p], 0.0)
-        fp[p, own] = rx[p, own] + above + below
+        over = jnp.where(row < DEPTH, qx[0, p], 0.0)
+        under = jnp.where(row >= 8 - DEPTH, qx[1, p], 0.0)
+        fp[p, own] = rx[p, centre_rows] + over + under
     late = halo(fp, (2,), 3) + onward(fp.at[0, own], tx, (), 3)
 
     for cp in scatter:
@@ -437,16 +485,15 @@
         cp.wait_recv()
     for j in range(8):
         lane = pl.ds(128 * j, 128)
-        cex[4:8, lane] = ch[8 + j]
-        cex[8:12, lane] = ce[j]
-        cex[12:16, lane] = ce[8 + j]
-        cex[16:20, lane] = ch[j]
+        cex[0:4, lane] = ce[j]
+        cex[4:8, lane] = ce[8 + j]
+        cex[8:12, lane] = ch[j]
+        cex[12:16, lane] = ch[8 + j]
     v = cex[...]
     w = v + fp[2]
-    ex[0] = (v - tx[...]) * jnp.exp(8.0 * cx[3])
+    ex[0] = (v - tx[...]) * inv[...]
     ex[1] = w
-    ex[2, own] = mid(decx[...] * w) + fp[1, own]
-    stores = []
+    ex[2, own] = dec * mid(w) + fp[1, own]
 
     def finish(b, carry):
         e = ex[b]
@@ -463,12 +510,9 @@
         ob[k + 5] += e + 6.0 * a1 + 8.0 * a2
         ob[k + 6] += e + 7.0 * a1 + 14.0 * a2 + 8.0 * a3
         ob[k + 7] += ex[b + 1, own]
-        pltpu.make_async_copy(ob.at[pl.ds(k, 8)], out.at[pl.ds(k, 8)], lsem.at[b]).start()
         return carry
 
     lax.fori_loop(0, 2, finish, 0)
-    for b in range(2):
-        pltpu.make_async_copy(ob.at[pl.ds(8 * b, 8)], out.at[pl.ds(8 * b, 8)], lsem.at[b]).wait()
     for cp in gather:
         cp.total.wait_send()
 
@@ -476,7 +520,8 @@
 def body(slabs, strips, u_coarse_guess, forcing, u_init, diffuse, vel_x, vel_y, react):
     points, rows, cols = u_coarse_guess.shape
     wide = rows + 2 * PAD
-    copies = 2 + 4 + 3 + 3 + 2 + 10 + 3 + 2 + 3 + 1 + 2 + 2
+    around = rows + 2 * NEAR
+    copies = 4 + 4 + 3 + 3 + 2 + 10 + 3 + 2 + 3 + 1 + 2 + 2
     f32 = jnp.float32
 
     def vmem(*shape):
@@ -484,25 +529,29 @@
 
     return pl.pallas_call(
         functools.partial(kernel, slabs, strips),
-        out_shape=jax.ShapeDtypeStruct(forcing.shape, f32),
+        out_shape=pltpu.VMEM(forcing.shape, f32),
         in_specs=[pl.BlockSpec(memory_space=pltpu.HBM)] * 7,
-        out_specs=pl.BlockSpec(memory_space=pl.ANY),
+        out_specs=pl.BlockSpec(memory_space=pltpu.VMEM),
         scratch_shapes=[
-            vmem(points + 1, wide, cols),
-            vmem(points, wide, cols),
+            vmem(points + 1, around, cols),
+            vmem(points, around, cols),
             vmem(points, rows, cols),
-            vmem(4, wide, cols),
+            vmem(4, rows, cols),
+            vmem(4, rows, cols),
+            vmem(4, rows, cols),
             vmem(5, wide, cols),
+            vmem(5, around, cols),
+            vmem(around, cols),
+            vmem(3, around, cols),
             vmem(wide, cols),
             vmem(3, DEPTH + 1, rows, cols),
-            vmem(points + 1, wide, cols),
-            vmem(points + 1, wide, cols),
+            vmem(points + 1, around, cols),
+            vmem(points + 1, around, cols),
             vmem(3, wide, cols),
             vmem(2, 3, rows, cols),
-            vmem(3, wide, cols),
-            vmem(wide, cols),
-            vmem(3, wide, cols),
-            vmem(2 * points, rows, cols),
+            vmem(3, around, cols),
+            vmem(around, cols),
+            vmem(3, around, cols),
             vmem(rows, cols),
             vmem(rows, cols),
             vmem(rows, cols),
@@ -515,7 +564,7 @@
             vmem(GROUP, 4, 128),
             vmem(GROUP, 4, 128),
             vmem(GROUP, 4, 128),
-            vmem(wide, cols),
+            vmem(around, cols),
             pltpu.SemaphoreType.DMA((8,)),
             pltpu.SemaphoreType.DMA((copies,)),
             pltpu.SemaphoreType.DMA((copies,)),

time: 44 us -> 40.9 us (0.930)
  Pallas kernels: 41.9 us -> 40 us
  local copies, waits for them, and re-layouts: 1.89 us -> 0.8 us
    pallas_call x1, Pallas kernels: 41.9 us -> 40 us  [body(): pl.pallas_call(functools.partial(kernel, slabs, strips), out_shape=pltpu....]
    unnamed x1, local copies, waits for them, and re-layouts: 1.89 us -> 0.8 us
where the time goes in v2:
time: 40.9 us; the launch traced here: 40.8 us
  Pallas kernels  40 us (98%)
  local copies, waits for them, and re-layouts  0.8 us (2%)
    pallas_call x1, Pallas kernels, body(): pl.pallas_call(functools.partial(kernel, slabs, strips), out_shape=pltpu....  40 us

profile of v2, /device:TPU:1, one launch (start us, length us, event | category | flops | bytes accessed | tf_op | source)
XLA Modules:
  0.0 40.8 jit_solution(9616323360441703758)
XLA Ops:
  0.0 40.0 %shard_map.73 = f32[16,8,1024]{2,1,0:T(8,128)S(1)} custom-call(f32[8,8,1024]{2,1,0:T(8,128)} %guess.1, f32[8,2,8,1024]{3,2,1,0:T(8,128)} %bitcast.1, f32[8,1024]{1,0:T(8,128)} %init.1, f32[8,1024]{1,0:T(8,128)} %diffuse.1, f32[8,1024]{1,0:T(8,128)} %vel_x.1, f32[8,1024]{1,0:T(8,128)} %vel_y.1, f32[8,1024]{1,0:T(8,128)} %react.1), custom_call_target="tpu_custom_call" | custom-call | flops 10000000 | bytes 1500000 | tf_op jit(solution)/shard_map/pallas_call | solution.py:530
  40.0 0.8 %copy.9 = f32[16,8,1024]{2,1,0:T(8,128)} copy(f32[16,8,1024]{2,1,0:T(8,128)S(1)} %shard_map.73) | data formatting | bytes 1048576

commit v3 on v2

--- a/solution.py
+++ b/solution.py
@@ -77,6 +77,7 @@
     lsem,
     ss,
     sr,
+    known,
 ):
     tm = lax.axis_index("tm")
     sx = lax.axis_index("space")
@@ -91,15 +92,24 @@
     own = pl.ds(0, 8)
     centre_rows = pl.ds(PAD, 8)
 
+    zc = q // 2
+    core = lax.rem(q, 2)
+    depth = GROUP // 2
+
+    def along_z(m, c):
+        return y * GROUP + lax.rem(zc + m + depth, depth) * 2 + c
+
+    def along_y(m):
+        return lax.rem(y + m + slabs, slabs) * GROUP + q
+
     barrier = pltpu.get_barrier_semaphore()
-    peers = [(tm, s) for s in xs]
-    for t in (nxt, prv):
-        peers += [(t, s) for s in (sx,) + xs]
-    for m in range(1, GROUP):
-        t = y * GROUP + lax.rem(q + m, GROUP)
-        peers += [(t, s) for s in (sx,) + xs]
-    for m in range(1, slabs):
-        peers.append((lax.rem(y + m, slabs) * GROUP + q, sx))
+    peers = [(tm, s) for s in xs] + [(nxt, sx), (prv, sx)]
+    for s in (sx,) + xs:
+        peers.append((along_z(0, 1 - core), s))
+        for m in (-2, -1, 1, 2):
+            peers += [(along_z(m, 0), s), (along_z(m, 1), s)]
+    for m in (-2, -1, 1, 2):
+        peers.append((along_y(m), sx))
     for dev in peers:
         pl.semaphore_signal(barrier, inc=1, device_id=dev, device_id_type=MESH)
 
@@ -250,6 +260,9 @@
         lax.fori_loop(0, cols // 128, one, 0)
 
     pl.semaphore_wait(barrier, len(peers))
+    word = [along_z(-2, core), along_z(2, core), along_y(-2), along_y(2), prv]
+    for dev in word:
+        pl.semaphore_signal(known, inc=1, device_id=(dev, sx), device_id_type=MESH)
 
     def parameters(dst, up, down, n):
         return [
@@ -261,7 +274,6 @@
     far = parameters(cf, 8 - DEPTH, NEAR, DEPTH - NEAR)
     early = halo(gx, (pl.ds(1, 7),), 2) + halo(fx, (slice(None),), 1)
     combine(0, first)
-    early += onward(g7, gx, (0,), 2)
     combine(1, second)
     combine(2, third)
 
@@ -290,6 +302,8 @@
     decx[8:16] = jnp.exp(-8.0 * raw[3])
     inv[0:8] = jnp.exp(8.0 * raw[3])
 
+    pl.semaphore_wait(known, len(word))
+    early += onward(g7, gx, (0,), 2)
     for cp in near:
         cp.wait_recv()
     raw = [cn[i] for i in range(4)]
@@ -568,6 +582,7 @@
             pltpu.SemaphoreType.DMA((8,)),
             pltpu.SemaphoreType.DMA((copies,)),
             pltpu.SemaphoreType.DMA((copies,)),
+            pltpu.SemaphoreType.REGULAR,
         ],
         compiler_params=pltpu.CompilerParams(
             collective_id=0, has_side_effects=True, vmem_limit_bytes=60 << 20

time: 40.9 us -> 40.6 us (level)
  no operation moved by 1% of the time
where the time goes in v3:
time: 40.6 us; the launch traced here: 40.5 us
  Pallas kernels  39.7 us (98%)
  local copies, waits for them, and re-layouts  0.8 us (2%)
    pallas_call x1, Pallas kernels, body(): pl.pallas_call(functools.partial(kernel, slabs, strips), out_shape=pltpu....  39.7 us

profile of v3, /device:TPU:1, one launch (start us, length us, event | category | flops | bytes accessed | tf_op | source)
XLA Modules:
  0.0 40.5 jit_solution(4444085508524455512)
XLA Ops:
  0.0 39.7 %shard_map.73 = f32[16,8,1024]{2,1,0:T(8,128)S(1)} custom-call(f32[8,8,1024]{2,1,0:T(8,128)} %guess.1, f32[8,2,8,1024]{3,2,1,0:T(8,128)} %bitcast.1, f32[8,1024]{1,0:T(8,128)} %init.1, f32[8,1024]{1,0:T(8,128)} %diffuse.1, f32[8,1024]{1,0:T(8,128)} %vel_x.1, f32[8,1024]{1,0:T(8,128)} %vel_y.1, f32[8,1024]{1,0:T(8,128)} %react.1), custom_call_target="tpu_custom_call" | custom-call | flops 10000000 | bytes 1500000 | tf_op jit(solution)/shard_map/pallas_call | solution.py:544
  39.7 0.8 %copy.9 = f32[16,8,1024]{2,1,0:T(8,128)} copy(f32[16,8,1024]{2,1,0:T(8,128)S(1)} %shard_map.73) | data formatting | bytes 1048576

commit v4 on v3

--- a/solution.py
+++ b/solution.py
@@ -60,7 +60,6 @@
     qx,
     fp,
     tx,
-    ex,
     ini,
     g7,
     d7,
@@ -311,15 +310,16 @@
         wn[i, 8:16] = v
     inv[8:16] = jnp.exp(8.0 * raw[3])
 
+    def stencils(w, values):
+        n = values[0].shape[0]
+        total = [w[4] * v for v in values]
+        for i, shift, axis in ((0, 1, 1), (1, cols - 1, 1), (2, 1, 0), (3, n - 1, 0)):
+            weight = w[i]
+            total = [t + weight * pltpu.roll(v, shift, axis) for t, v in zip(total, values)]
+        return total
+
     def stencil(w, v):
-        n = v.shape[0]
-        return (
-            w[4] * v
-            + w[0] * pltpu.roll(v, 1, 1)
-            + w[1] * pltpu.roll(v, cols - 1, 1)
-            + w[2] * pltpu.roll(v, 1, 0)
-            + w[3] * pltpu.roll(v, n - 1, 0)
-        )
+        return stencils(w, [v])[0]
 
     def ap(v):
         return stencil(wn, v)
@@ -331,20 +331,22 @@
         none = jnp.zeros_like(v)
         return jnp.concatenate([none, v, none], axis=0)
 
-    def horner_near(p, carry):
-        top = DEPTH - p // 2
-
-        def start(m):
-            v = px[p, m]
-            return jnp.concatenate([v, jnp.zeros_like(v)], axis=0)
-
-        def level(i, v):
-            return ap(v) + start(top - 1 - i)
-
-        rn[p] = lax.fori_loop(0, NEAR, level, start(top))
+    tops = (DEPTH, DEPTH, DEPTH - 1)
+
+    def start(p, m):
+        v = px[p, m]
+        return jnp.concatenate([v, jnp.zeros_like(v)], axis=0)
+
+    for p in range(3):
+        rn[p] = start(p, tops[p])
+
+    def level_near(i, carry):
+        new = stencils(wn, [rn[p] for p in range(3)])
+        for p in range(3):
+            rn[p] = new[p] + start(p, tops[p] - 1 - i)
         return carry
 
-    lax.fori_loop(0, 3, horner_near, 0)
+    lax.fori_loop(0, NEAR, level_near, 0)
 
     for cp in far:
         cp.wait_recv()
@@ -354,18 +356,14 @@
             wx[i, 8 * t : 8 * t + 8] = v
         decx[8 * t : 8 * t + 8] = jnp.where(inside, jnp.exp(-8.0 * raw[3]), 0.0)
 
-    def horner_far(p, carry):
-        top = DEPTH - p // 2
-
-        def level(i, v):
-            return stencil(wx, v) + around(px[p, top - 1 - NEAR - i])
-
+    for p in range(3):
         v = rn[p, 8:16]
-        v = jnp.concatenate([jnp.where(low, 0.0, v), rn[p, 0:8], jnp.where(low, v, 0.0)], axis=0)
-        rx[p] = lax.fori_loop(0, top - NEAR, level, v)
-        return carry
-
-    lax.fori_loop(0, 3, horner_far, 0)
+        rx[p] = jnp.concatenate([jnp.where(low, 0.0, v), rn[p, 0:8], jnp.where(low, v, 0.0)], axis=0)
+    for i in range(NEAR, DEPTH):
+        left = [p for p in range(3) if i < tops[p]]
+        new = stencils(wx, [rx[p] for p in left])
+        for p in left:
+            rx[p] = new[p] + around(px[p, tops[p] - 1 - i])
 
     decv = decx[...]
     dec = decv[8:16]
@@ -505,28 +503,26 @@
         cex[12:16, lane] = ch[8 + j]
     v = cex[...]
     w = v + fp[2]
-    ex[0] = (v - tx[...]) * inv[...]
-    ex[1] = w
-    ex[2, own] = dec * mid(w) + fp[1, own]
-
-    def finish(b, carry):
-        e = ex[b]
-        a1 = ap(e)
-        a2 = ap(a1)
-        a3 = mid(ap(a2))
-        e, a1, a2 = mid(e), mid(a1), mid(a2)
+    ends = [(v - tx[...]) * inv[...], w]
+    a1 = stencils(wn, ends)
+    a2 = stencils(wn, a1)
+    a3 = [mid(v) for v in stencils(wn, a2)]
+    ends = [mid(v) for v in ends]
+    a1 = [mid(v) for v in a1]
+    a2 = [mid(v) for v in a2]
+    ends.append(dec * ends[1] + fp[1, own])
+    for b in range(2):
+        e, p1, p2, p3 = ends[b], a1[b], a2[b], a3[b]
         k = 8 * b
-        ob[k] += e + a1
-        ob[k + 1] += e + 2.0 * a1
-        ob[k + 2] += e + 3.0 * a1 + 2.0 * a2
-        ob[k + 3] += e + 4.0 * a1
-        ob[k + 4] += e + 5.0 * a1 + 4.0 * a2
-        ob[k + 5] += e + 6.0 * a1 + 8.0 * a2
-        ob[k + 6] += e + 7.0 * a1 + 14.0 * a2 + 8.0 * a3
-        ob[k + 7] += ex[b + 1, own]
-        return carry
-
-    lax.fori_loop(0, 2, finish, 0)
+        ob[k] += e + p1
+        ob[k + 1] += e + 2.0 * p1
+        ob[k + 2] += e + 3.0 * p1 + 2.0 * p2
+        ob[k + 3] += e + 4.0 * p1
+        ob[k + 4] += e + 5.0 * p1 + 4.0 * p2
+        ob[k + 5] += e + 6.0 * p1 + 8.0 * p2
+        ob[k + 6] += e + 7.0 * p1 + 14.0 * p2 + 8.0 * p3
+        ob[k + 7] += ends[b + 1]
+
     for cp in gather:
         cp.total.wait_send()
 
@@ -565,7 +561,6 @@
             vmem(2, 3, rows, cols),
             vmem(3, around, cols),
             vmem(around, cols),
-            vmem(3, around, cols),
             vmem(rows, cols),
             vmem(rows, cols),
             vmem(rows, cols),

time: 40.6 us -> 39.5 us (0.973)
  Pallas kernels: 39.7 us -> 38.6 us
    pallas_call x1, Pallas kernels: 39.7 us -> 38.6 us  [body(): pl.pallas_call(functools.partial(kernel, slabs, strips), out_shape=pltpu....]
where the time goes in v4:
time: 39.5 us; the launch traced here: 39.4 us
  Pallas kernels  38.6 us (98%)
  local copies, waits for them, and re-layouts  0.8 us (2%)
    pallas_call x1, Pallas kernels, body(): pl.pallas_call(functools.partial(kernel, slabs, strips), out_shape=pltpu....  38.6 us
    unnamed x1, local copies, waits for them, and re-layouts  0.8 us

profile of v4, /device:TPU:1, one launch (start us, length us, event | category | flops | bytes accessed | tf_op | source)
XLA Modules:
  0.0 39.4 jit_solution(9200754544567950994)
XLA Ops:
  0.0 38.6 %shard_map.73 = f32[16,8,1024]{2,1,0:T(8,128)S(1)} custom-call(f32[8,8,1024]{2,1,0:T(8,128)} %guess.1, f32[8,2,8,1024]{3,2,1,0:T(8,128)} %bitcast.1, f32[8,1024]{1,0:T(8,128)} %init.1, f32[8,1024]{1,0:T(8,128)} %diffuse.1, f32[8,1024]{1,0:T(8,128)} %vel_x.1, f32[8,1024]{1,0:T(8,128)} %vel_y.1, f32[8,1024]{1,0:T(8,128)} %react.1), custom_call_target="tpu_custom_call" | custom-call | flops 10000000 | bytes 1500000 | tf_op jit(solution)/shard_map/pallas_call | solution.py:540
  38.6 0.8 %copy.9 = f32[16,8,1024]{2,1,0:T(8,128)} copy(f32[16,8,1024]{2,1,0:T(8,128)S(1)} %shard_map.73) | data formatting | bytes 1048576

commit v5 on v4

--- a/solution.py
+++ b/solution.py
@@ -46,6 +46,7 @@
     fx,
     hx,
     cx,
+    cb,
     cn,
     cf,
     wx,
@@ -269,7 +270,8 @@
             send(cx.at[:, pl.ds(down, n)], dst.at[:, pl.ds(down, n)], (tm, xs[1])),
         ]
 
-    near = parameters(cn, 8 - NEAR, 0, NEAR)
+    closest = parameters(cb, 6, 0, 2)
+    near = parameters(cn, 4, 2, 2)
     far = parameters(cf, 8 - DEPTH, NEAR, DEPTH - NEAR)
     early = halo(gx, (pl.ds(1, 7),), 2) + halo(fx, (slice(None),), 1)
     combine(0, first)
@@ -301,14 +303,13 @@
     decx[8:16] = jnp.exp(-8.0 * raw[3])
     inv[0:8] = jnp.exp(8.0 * raw[3])
 
-    pl.semaphore_wait(known, len(word))
-    early += onward(g7, gx, (0,), 2)
-    for cp in near:
-        cp.wait_recv()
-    raw = [cn[i] for i in range(4)]
-    for i, v in enumerate(weights(raw, (low & beneath) | (~low & above), None, None)):
+    for cp in closest:
+        cp.wait_recv()
+    beside = (low & beneath) | (~low & above)
+    two = (row < 2) | (row >= 6)
+    raw = [cb[i] for i in range(4)]
+    for i, v in enumerate(weights(raw, beside & two, None, None)):
         wn[i, 8:16] = v
-    inv[8:16] = jnp.exp(8.0 * raw[3])
 
     def stencils(w, values):
         n = values[0].shape[0]
@@ -346,12 +347,18 @@
             rn[p] = new[p] + start(p, tops[p] - 1 - i)
         return carry
 
-    lax.fori_loop(0, NEAR, level_near, 0)
+    lax.fori_loop(0, 2, level_near, 0)
+    for cp in near:
+        cp.wait_recv()
+    four = [jnp.where(two, cb[i], cn[i]) for i in range(4)]
+    for i, v in enumerate(weights(four, beside, None, None)):
+        wn[i, 8:16] = v
+    lax.fori_loop(2, NEAR, level_near, 0)
 
     for cp in far:
         cp.wait_recv()
     for t, inside in ((0, (row >= PAD - DEPTH) & above), (2, (row < DEPTH) & beneath)):
-        raw = [jnp.where(low, cn[i] if t else cf[i], cf[i] if t else cn[i]) for i in range(4)]
+        raw = [jnp.where(low, four[i] if t else cf[i], cf[i] if t else four[i]) for i in range(4)]
         for i, v in enumerate(weights(raw, inside, None, None)):
             wx[i, 8 * t : 8 * t + 8] = v
         decx[8 * t : 8 * t + 8] = jnp.where(inside, jnp.exp(-8.0 * raw[3]), 0.0)
@@ -375,6 +382,8 @@
             for t in range(3):
                 r = 8 * t + 4 * h
                 sp[t, 8 * h + j] = part[r : r + 4, 128 * j : 128 * j + 128]
+
+    pl.semaphore_wait(known, len(word))
 
     def mate(m):
         to = lax.rem(q + m, GROUP)
@@ -393,6 +402,8 @@
         send(rx.at[:, pl.ds(16, DEPTH)], qx.at[0, :, pl.ds(0, DEPTH)], (tm, xs[0])),
         send(rx.at[:, pl.ds(8 - DEPTH, DEPTH)], qx.at[1, :, pl.ds(8 - DEPTH, DEPTH)], (tm, xs[1])),
     ]
+    early += onward(g7, gx, (0,), 2)
+    inv[8:16] = jnp.exp(8.0 * four[3])
     d1 = dp[q]
     d2 = d1 * d1
 
@@ -531,7 +542,7 @@
     points, rows, cols = u_coarse_guess.shape
     wide = rows + 2 * PAD
     around = rows + 2 * NEAR
-    copies = 4 + 4 + 3 + 3 + 2 + 10 + 3 + 2 + 3 + 1 + 2 + 2
+    copies = 6 + 4 + 3 + 3 + 2 + 10 + 3 + 2 + 3 + 1 + 2 + 2
     f32 = jnp.float32
 
     def vmem(*shape):
@@ -546,6 +557,7 @@
             vmem(points + 1, around, cols),
             vmem(points, around, cols),
             vmem(points, rows, cols),
+            vmem(4, rows, cols),
             vmem(4, rows, cols),
             vmem(4, rows, cols),
             vmem(4, rows, cols),

time: 39.5 us -> 39.4 us (level)
  no operation moved by 1% of the time
where the time goes in v5:
time: 39.4 us; the launch traced here: 39.3 us
  Pallas kernels  38.5 us (98%)
  local copies, waits for them, and re-layouts  0.8 us (2%)
    pallas_call x1, Pallas kernels, body(): pl.pallas_call(functools.partial(kernel, slabs, strips), out_shape=pltpu....  38.5 us
    unnamed x1, local copies, waits for them, and re-layouts  0.8 us

profile of v5, /device:TPU:1, one launch (start us, length us, event | category | flops | bytes accessed | tf_op | source)
XLA Modules:
  0.0 39.3 jit_solution(14942159373565576450)
XLA Ops:
  0.0 38.5 %shard_map.73 = f32[16,8,1024]{2,1,0:T(8,128)S(1)} custom-call(f32[8,8,1024]{2,1,0:T(8,128)} %guess.1, f32[8,2,8,1024]{3,2,1,0:T(8,128)} %bitcast.1, f32[8,1024]{1,0:T(8,128)} %init.1, f32[8,1024]{1,0:T(8,128)} %diffuse.1, f32[8,1024]{1,0:T(8,128)} %vel_x.1, f32[8,1024]{1,0:T(8,128)} %vel_y.1, f32[8,1024]{1,0:T(8,128)} %react.1), custom_call_target="tpu_custom_call" | custom-call | flops 10000000 | bytes 1500000 | tf_op jit(solution)/shard_map/pallas_call | solution.py:551
  38.5 0.8 %copy.9 = f32[16,8,1024]{2,1,0:T(8,128)} copy(f32[16,8,1024]{2,1,0:T(8,128)S(1)} %shard_map.73) | data formatting | bytes 1048576

commit v6 on v5

--- a/solution.py
+++ b/solution.py
@@ -259,6 +259,9 @@
 
         lax.fori_loop(0, cols // 128, one, 0)
 
+    combine(0, first)
+    combine(1, second)
+    combine(2, third)
     pl.semaphore_wait(barrier, len(peers))
     word = [along_z(-2, core), along_z(2, core), along_y(-2), along_y(2), prv]
     for dev in word:
@@ -274,9 +277,6 @@
     near = parameters(cn, 4, 2, 2)
     far = parameters(cf, 8 - DEPTH, NEAR, DEPTH - NEAR)
     early = halo(gx, (pl.ds(1, 7),), 2) + halo(fx, (slice(None),), 1)
-    combine(0, first)
-    combine(1, second)
-    combine(2, third)
 
     row = lax.broadcasted_iota(jnp.int32, (8, cols), 0)
     col = lax.broadcasted_iota(jnp.int32, (8, cols), 1)

time: 39.4 us -> 39.4 us (level)
  no operation moved by 1% of the time
where the time goes in v6:
time: 39.4 us; the launch traced here: 39.3 us
  Pallas kernels  38.5 us (98%)
  local copies, waits for them, and re-layouts  0.8 us (2%)
    pallas_call x1, Pallas kernels, body(): pl.pallas_call(functools.partial(kernel, slabs, strips), out_shape=pltpu....  38.5 us
    unnamed x1, local copies, waits for them, and re-layouts  0.8 us

profile of v6, /device:TPU:1, one launch (start us, length us, event | category | flops | bytes accessed | tf_op | source)
XLA Modules:
  0.0 39.3 jit_solution(7124476790632371170)
XLA Ops:
  0.0 38.5 %shard_map.73 = f32[16,8,1024]{2,1,0:T(8,128)S(1)} custom-call(f32[8,8,1024]{2,1,0:T(8,128)} %guess.1, f32[8,2,8,1024]{3,2,1,0:T(8,128)} %bitcast.1, f32[8,1024]{1,0:T(8,128)} %init.1, f32[8,1024]{1,0:T(8,128)} %diffuse.1, f32[8,1024]{1,0:T(8,128)} %vel_x.1, f32[8,1024]{1,0:T(8,128)} %vel_y.1, f32[8,1024]{1,0:T(8,128)} %react.1), custom_call_target="tpu_custom_call" | custom-call | flops 10000000 | bytes 1500000 | tf_op jit(solution)/shard_map/pallas_call | solution.py:551
  38.5 0.8 %copy.9 = f32[16,8,1024]{2,1,0:T(8,128)} copy(f32[16,8,1024]{2,1,0:T(8,128)S(1)} %shard_map.73) | data formatting | bytes 1048576
